TPU v7x, 32 devices: a whole 2x2x4 slice. The times are simulated.
32 devices in a mesh: dp: 8 (over y, x, core), tensor: 4 (over z).
Axes of the slice: x: 2, y: 2, z: 4, core: 2. Of those that a mesh axis runs over, the one named last changes fastest.
Arguments:
- acts: bfloat16 [256, 4096], P(('dp', 'tensor')), may hold values from -6 to 6
- gate_pre: bfloat16 [256, 14336], P('dp', 'tensor'), may hold values from -8 to 8
- up_pre: bfloat16 [256, 14336], P('dp', 'tensor'), may hold values from -6 to 6
- out_grad: bfloat16 [256, 4096], P(('dp', 'tensor')), may hold values from -6 to 6
- segments: int32 [8, 32], P('dp', 'tensor'), may hold values from 0 to 23, never falling along the last dimension, each value on 1 to 8 neighbouring positions
- down_weight: bfloat16 [4096, 14336], P(None, 'tensor'), may hold values from -0.046875 to 0.046875
Outputs:
- grad_gate: float32 [4096, 14336], P('dp', 'tensor')
- grad_up: float32 [4096, 14336], P('dp', 'tensor')
- grad_down: float32 [4096, 14336], P('dp', 'tensor')
Inputs may be any that keep to these rules, and one draw needn't show every extreme that they name: `segments`: within each group ids never fall; each id that occurs covers 1 to 8 tokens, and some id covers exactly that many.
All inputs are finite; a program needn't handle non-finite values.
Results may differ from a plain program's by a relative error of at most 0.014.
Values may be sent and summed in bfloat16 or wider, within the bound.
A program may use at most 256 MiB of HBM per device.

v0:
```python
import jax
import jax.numpy as jnp
from jax import lax
from jax.sharding import PartitionSpec as P

MESH = ("dp", "tensor")


def contract(left, right):
    return lax.dot_general(
        left, right, (((0,), (0,)), ((), ())), preferred_element_type=jnp.float32
    )


def token_weights(seg_groups):
    same = seg_groups[:, :, None] == seg_groups[:, None, :]
    return 1.0 / jnp.sum(same.astype(jnp.float32), axis=2).reshape(-1)


def body(acts, gate_pre, up_pre, out_grad, segments, down_weight):
    n_dp, n_t = lax.axis_size("dp"), lax.axis_size("tensor")
    rows, d = acts.shape
    grad_all = lax.all_gather(out_grad, MESH, axis=0, tiled=True)
    gate_all = lax.all_gather(gate_pre, "dp", axis=0, tiled=True)
    up_all = lax.all_gather(up_pre, "dp", axis=0, tiled=True)
    seg_all = lax.all_gather(segments, MESH, axis=0, tiled=True)
    seg_all = seg_all.reshape(n_dp, n_t * rows)
    cols = d // n_dp
    mine = lax.all_to_all(acts, "dp", split_axis=1, concat_axis=0, tiled=True)
    mine = lax.all_gather(mine, "tensor", axis=0, tiled=False)
    mine = mine.reshape(n_t, n_dp, rows, cols).transpose(1, 0, 2, 3).reshape(-1, cols)
    me = lax.axis_index("dp")
    grad_mine = lax.dynamic_slice_in_dim(grad_all, me * cols, cols, axis=1)
    weights = token_weights(seg_all)[:, None]
    raw = jnp.dot(grad_all, down_weight, preferred_element_type=jnp.float32)
    gate = gate_all.astype(jnp.float32)
    up = up_all.astype(jnp.float32)
    sigma = jax.nn.sigmoid(gate)
    active = gate * sigma
    hidden_grad = weights * raw
    gate_grad = (hidden_grad * up * sigma * (1.0 + gate * (1.0 - sigma))).astype(jnp.bfloat16)
    up_grad = (hidden_grad * active).astype(jnp.bfloat16)
    weighted_hidden = (weights * active * up).astype(jnp.bfloat16)
    return contract(mine, gate_grad), contract(mine, up_grad), contract(grad_mine, weighted_hidden)


def solution(mesh):
    in_specs = (
        P(("dp", "tensor"), None),
        P("dp", "tensor"),
        P("dp", "tensor"),
        P(("dp", "tensor"), None),
        P("dp", "tensor"),
        P(None, "tensor"),
    )
    out_specs = (P("dp", "tensor"), P("dp", "tensor"), P("dp", "tensor"))
    return jax.shard_map(body, mesh=mesh, in_specs=in_specs, out_specs=out_specs, check_vma=False)
```

profile of v0, /device:TPU:0, one launch (start us, length us, event | category | flops | bytes accessed | tf_op | source)
XLA Modules:
  0.0 171.2 jit_solution(6032649243486719504)
XLA Ops:
  7.2 0.0 all-gather.5.cloned.1.call-start
  7.2 0.7 all-gather.5.cloned.1.call-update
  7.9 0.0 all-gather.7.cloned.1.call-start
  7.9 0.7 all-gather.7.cloned.1.call-update
  8.6 0.0 all-gather.9.cloned.1.call-start
  8.7 0.7 all-gather.9.cloned.1.call-update
  9.4 5.2 %all-to-all-start = ((bf16[8,8,512]{2,0,1:T(8,128)(2,1)}), bf16[8,8,512]{2,0,1:T(8,128)(2,1)S(1)}, u32[]{:S(2)}, u32[]{:S(2)}) async-start(bf16[8,8,512]{2,0,1:T(8,128)(2,1)} %bitcast.21), calls=%async_computation | async-start | bytes 131072 | tf_op jit(solution)/shard_map/all_to_all | solution.py:29
  14.6 68.9 %all-gather = s32[32,1,8]{2,1,0:T(1,128)S(1)} all-gather(s32[1,1,8]{2,1,0:T(1,128)} %bitcast.22), channel_id=1, replica_groups=mesh['dp'=8,'tensor'=4] {'dp','tensor'}, dimensions={0}, use_global_device_ids=true | all-gather | bytes 1056 | tf_op jit(solution)/shard_map/all_gather | solution.py:26
  83.5 0.5 broadcast.24
  84.0 0.7 reduce.3
  84.7 0.1 eq.15
  84.7 0.2 convert_reduce_fusion
  84.9 0.1 div.18
  85.0 0.0 all-to-all-done
  85.0 14.2 %all_gather.23 = bf16[4,64,512]{2,1,0:T(8,128)(2,1)S(1)} all-gather(bf16[1,64,512]{2,1,0:T(8,128)(2,1)S(1)} %bitcast.18), channel_id=1, replica_groups=mesh['dp'=8,'tensor'=4] {'tensor'}, dimensions={0}, use_global_device_ids=true | all-gather | bytes 327680 | tf_op jit(solution)/shard_map/all_gather | solution.py:30
  99.2 0.0 all-gather.5.cloned.1.call-done
  99.3 15.4 %convolution_multiply_fusion = f32[256,3584]{1,0:T(8,128)} fusion(bf16[256,4096]{1,0:T(8,128)(2,1)} %all-gather.5.cloned.1.call-done, bf16[4096,3584]{1,0:T(8,128)(2,1)} %param.11, f32[256]{0:T(256)S(1)} %div.18), kind=kOutput, calls=%fused_computation.2 | convolution fusion | flops 7517110272 | bytes 35128320 | tf_op jit(solution)/shard_map/dot_general | solution.py:35
  114.7 11.8 %all-gather.9.cloned.1.call-done = bf16[256,3584]{1,0:T(8,128)(2,1)} async-done(((bf16[32,3584]{1,0:T(8,128)(2,1)}), bf16[256,3584]{1,0:T(8,128)(2,1)}) %all-gather.9.cloned.1.call-update) | async-done | bytes 1835024 | tf_op jit(solution)/shard_map/all_gather | solution.py:24
  126.5 8.4 %convolution_bitcast_fusion.1 = f32[512,3584]{0,1:T(8,128)} fusion(bf16[256,512]{1,0:T(8,128)(2,1)S(1)} %bitcast.19, f32[256,3584]{1,0:T(8,128)} %convolution_multiply_fusion, bf16[256,3584]{1,0:T(8,128)(2,1)} %all-gather.7.cloned.1.call-done, bf16[256,3584]{1,0:T(8,128)(2,1)} %all-gather.9.cloned.1.call-done), kind=kOutput, calls=%fused_computation.1 | convolution fusion | flops 950534144 | bytes 14942208 | tf_op jit(solution)/shard_map/dot_general | solution.py:10
  134.9 8.5 %copy.20 = f32[512,3584]{1,0:T(8,128)} copy(f32[512,3584]{0,1:T(8,128)} %convolution_bitcast_fusion.1) | data formatting | bytes 14680064
  143.4 0.0 copy-done.1
  143.4 6.4 %convolution_bitcast_fusion = f32[512,3584]{0,1:T(8,128)} fusion(bf16[256,512]{1,0:T(8,128)(2,1)S(1)} %bitcast.20, f32[256,3584]{1,0:T(8,128)} %convolution_multiply_fusion, bf16[256,3584]{1,0:T(8,128)(2,1)S(1)} %copy-done.1), kind=kOutput, calls=%fused_computation | convolution fusion | flops 945946624 | bytes 13107200 | tf_op jit(solution)/shard_map/dot_general | solution.py:10
  149.8 8.5 %copy.21 = f32[512,3584]{1,0:T(8,128)} copy(f32[512,3584]{0,1:T(8,128)} %convolution_bitcast_fusion) | data formatting | bytes 14680064
  158.3 6.4 %fusion.8 = f32[512,3584]{1,0:T(8,128)} fusion(bf16[256,3584]{1,0:T(8,128)(2,1)S(1)} %copy-done, f32[256]{0:T(256)S(1)} %div.18, bf16[256,3584]{1,0:T(8,128)(2,1)} %all-gather.9.cloned.1.call-done, bf16[256,4096]{1,0:T(8,128)(2,1)} %all-gather.5.cloned.1.call-done, s32[]{:T(128)S(6)} %select_n.3), kind=kOutput, calls=%fused_computation.17 | convolution fusion | flops 947781632 | bytes 11273220 | tf_op jit(solution)/shard_map/dot_general | solution.py:10
  (6 shorter events, 0.0 us)
Async XLA Ops:
  7.2 92.1 %all-gather.5.cloned.1.call-start = ((), (), s32[]{:S(2)}) async-start(), calls=%async_computation.1 | async-start | bytes 2162688 | tf_op jit(solution)/shard_map/all_gather | solution.py:23
  7.9 106.8 %all-gather.7.cloned.1.call-start = ((), (), s32[]{:S(2)}) async-start(), calls=%async_computation.2 | async-start | bytes 2064384 | tf_op jit(solution)/shard_map/all_gather | solution.py:25
  8.6 117.8 %all-gather.9.cloned.1.call-start = ((), (), s32[]{:S(2)}) async-start(), calls=%async_computation.3 | async-start | bytes 2064384 | tf_op jit(solution)/shard_map/all_gather | solution.py:24
  9.4 75.6 %all-to-all-start = ((bf16[8,8,512]{2,0,1:T(8,128)(2,1)}), bf16[8,8,512]{2,0,1:T(8,128)(2,1)S(1)}, u32[]{:S(2)}, u32[]{:S(2)}) async-start(bf16[8,8,512]{2,0,1:T(8,128)(2,1)} %bitcast.21), calls=%async_computation | async-start | bytes 131072 | tf_op jit(solution)/shard_map/all_to_all | solution.py:29
  134.9 8.5 %copy-start.1 = (bf16[256,3584]{1,0:T(8,128)(2,1)S(1)}, bf16[256,3584]{1,0:T(8,128)(2,1)}, u32[]{:S(2)}) copy-start(bf16[256,3584]{1,0:T(8,128)(2,1)} %all-gather.9.cloned.1.call-done) | copy-start | bytes 5505028
  149.8 8.5 %copy-start = (bf16[256,3584]{1,0:T(8,128)(2,1)S(1)}, bf16[256,3584]{1,0:T(8,128)(2,1)}, u32[]{:S(2)}) copy-start(bf16[256,3584]{1,0:T(8,128)(2,1)} %all-gather.7.cloned.1.call-done) | copy-start | bytes 5505028
Sparse Core Ops, SparseCore 0:
  10.9 59.1 all-gather.4
  72.0 25.6 all-gather.6
  99.6 26.8 all-gather.8
where the time goes:
time: 172 us; the launch traced here: 171 us
  blocking collectives  83.1 us (48%)
  matrix products  36.6 us (21%)
  local copies, waits for them, and re-layouts  17.7 us (10%)
  waiting for transfers between devices  13.9 us (8%)
  between operations  13.8 us (8%)
  starting transfers between devices  5.3 us (3%)
    all_gather x1, blocking collectives, body(): seg_all = lax.all_gather(segments, MESH, axis=0, tiled=True)  68.9 us
    dot_general x3, matrix products, contract(): lax.dot_general(left, right, (((0,), (0,)), ((), ())), preferred_element_...  21.2 us
    unnamed x6, local copies, waits for them, and re-layouts  17 us
    dot_general x1, matrix products, body(): raw = jnp.dot(grad_all, down_weight, preferred_element_type=jnp.float32)  15.4 us
    all_gather x1, blocking collectives, body(): mine = lax.all_gather(mine, 'tensor', axis=0, tiled=False)  14.2 us
    all_gather x1, waiting for transfers between devices, body(): gate_all = lax.all_gather(gate_pre, 'dp', axis=0, tiled=True)  11.8 us
    all_to_all x1, starting transfers between devices, body(): mine = lax.all_to_all(acts, 'dp', split_axis=1, concat_axis=0, tiled=True)  5.18 us
  transfers between devices with their start and end apart: 4, of which 1 were waited for; matrix products, arithmetic and copies ran while one was open for 10% of the time, Pallas kernels for 0%

commit v1 on v0

--- a/solution.py
+++ b/solution.py
@@ -1,9 +1,368 @@
+import functools
+
 import jax
 import jax.numpy as jnp
 from jax import lax
+from jax.experimental import pallas as pl
+from jax.experimental.pallas import tpu as pltpu
 from jax.sharding import PartitionSpec as P
 
 MESH = ("dp", "tensor")
+F32, BF16 = jnp.float32, jnp.bfloat16
+CORE, NEAR, FAR = 1, 2, 4
+
+
+def tile_of(extent, most):
+    return max(t for t in range(128, most + 1, 128) if extent % t == 0)
+
+
+def hidden_kernel(
+    n_dp, n_t,
+    acts, grads, segs, gate_in, up_in, weight_in,
+    gg_out, ug_out, wh_out, acts_t_out, grads_t_out,
+    og, acts_cut, ac, sg, gu, wt, acc, lhs32, lhs16, own32, sg32, wgt,
+    og_s, og_r, line_s, line_r, sib_s, sib_r, cut_s, cut_r, cl_s, cl_r, gu_s, gu_r, w_sem, own_sem,
+):
+    chips = n_dp // 2
+    nk = chips
+    rows, d = acts.shape
+    dk = d // nk
+    half = dk // 2
+    group = n_t * rows
+    ff = gate_in.shape[1]
+    nf = gu.shape[1]
+    fcut = ff // nf
+    dp, z = lax.axis_index("dp"), lax.axis_index("tensor")
+    core, chip = dp % 2, dp // 2
+
+    def send(src, dst, s, r, to_dp, to_z):
+        pltpu.make_async_remote_copy(
+            src_ref=src, dst_ref=dst, send_sem=s, recv_sem=r,
+            device_id=(to_dp, to_z), device_id_type=pl.DeviceIdType.MESH,
+        ).start()
+
+    def desc(ref, s, r):
+        return pltpu.make_async_remote_copy(
+            src_ref=ref, dst_ref=ref, send_sem=s, recv_sem=r,
+            device_id=(dp ^ CORE, z), device_id_type=pl.DeviceIdType.MESH,
+        )
+
+    barrier = pltpu.get_barrier_semaphore()
+    for rel in range(1, n_dp):
+        pl.semaphore_signal(barrier, inc=1, device_id=(dp ^ rel, z), device_id_type=pl.DeviceIdType.MESH)
+
+    @pl.when(z > 0)
+    def _():
+        pl.semaphore_signal(barrier, inc=1, device_id=(dp, z - 1), device_id_type=pl.DeviceIdType.MESH)
+
+    @pl.when(z < n_t - 1)
+    def _():
+        pl.semaphore_signal(barrier, inc=1, device_id=(dp, z + 1), device_id_type=pl.DeviceIdType.MESH)
+
+    w_copies = [
+        pltpu.make_async_copy(weight_in.at[pl.ds(k * dk, dk)], wt.at[pl.ds(k * dk, dk)], w_sem.at[k])
+        for k in range(nk)
+    ]
+    for c in w_copies:
+        c.start()
+    gu_in = (gate_in, up_in)
+    own_copies = []
+    for j in range(2):
+        for f in range(nf):
+            c = pltpu.make_async_copy(gu_in[j].at[:, pl.ds(f * fcut, fcut)], gu.at[j, f, dp], own_sem.at[j, f])
+            c.start()
+            own_copies.append(c)
+
+    def stacked(x):
+        w = x.shape[1] // 2
+        return jnp.concatenate([x[:, :w], x[:, w:]], axis=0).astype(BF16)
+
+    for k in range(nk):
+        og[k, core, z, chip] = stacked(grads[:, k * dk:(k + 1) * dk].astype(F32))
+    cols = d // n_dp
+    for i in range(n_dp):
+        acts_cut[i] = stacked(acts[:, i * cols:(i + 1) * cols].astype(F32))
+    ac[z, dp] = acts_cut[dp]
+    seg_row = jnp.broadcast_to(segs[...], (rows, rows))
+    diag = lax.broadcasted_iota(jnp.int32, (rows, rows), 0) == lax.broadcasted_iota(jnp.int32, (rows, rows), 1)
+    seg_col = jnp.sum(jnp.where(diag, seg_row, 0), axis=1, keepdims=True)
+    sg[z, dp] = jnp.broadcast_to(seg_col, (rows, 128))
+
+    pl.semaphore_wait(barrier, n_dp - 1 + (z > 0).astype(jnp.int32) + (z < n_t - 1).astype(jnp.int32))
+
+    for k in range(nk):
+        for rel in range(1, chips):
+            mine = og.at[k, core, z, chip]
+            send(mine, mine, og_s.at[k, rel], og_r.at[k, rel], dp ^ (2 * rel), z)
+
+    def gu_axes(j):
+        return (NEAR, FAR) if j == 0 else (FAR, NEAR)
+
+    def start_gu():
+        for f in range(nf):
+            for j in range(2):
+                own_copies[j * nf + f].wait()
+            for t in range(2):
+                for j in range(2):
+                    mine = gu.at[j, f, dp]
+                    send(mine, mine, gu_s.at[j, f, t], gu_r.at[j, f, t], dp ^ gu_axes(j)[t], z)
+            for j in range(2):
+                mine = gu.at[j, f, dp]
+                send(mine, mine, gu_s.at[j, f, 3], gu_r.at[j, f, 3], dp ^ CORE, z)
+
+    def gu_hop(j, f, t):
+        a, b = gu_axes(j)
+        slot = gu.at[j, f, dp ^ (a, b, a ^ b)[t]]
+        desc(slot, gu_s.at[j, f, t], gu_r.at[j, f, t]).wait_recv()
+        if t == 0:
+            send(slot, slot, gu_s.at[j, f, 2], gu_r.at[j, f, 2], dp ^ b, z)
+        send(slot, slot, gu_s.at[j, f, 4 + t], gu_r.at[j, f, 4 + t], dp ^ CORE, z)
+
+    def start_cut():
+        for rel in range(1, n_dp):
+            send(acts_cut.at[dp ^ rel], ac.at[z, dp], cut_s.at[0, rel], cut_r.at[0, rel], dp ^ rel, z)
+            send(sg.at[z, dp], sg.at[z, dp], cut_s.at[1, rel], cut_r.at[1, rel], dp ^ rel, z)
+
+    def line_parts(k):
+        if k < nk:
+            return [(lambda s: og.at[k, core, s], line_s.at[k], line_r.at[k])]
+        return [(lambda s: ac.at[s], cl_s.at[0], cl_r.at[0]), (lambda s: sg.at[s], cl_s.at[1], cl_r.at[1])]
+
+    def pass_on(k, s):
+        if k < nk:
+            plane = og.at[k, core, s]
+            send(plane, plane, sib_s.at[k, s], sib_r.at[k, s], dp ^ CORE, z)
+
+    def step(k, h):
+        if h == 0:
+            if k < nk:
+                for rel in range(1, chips):
+                    desc(og.at[k, core, z, chip ^ rel], og_s.at[k, rel], og_r.at[k, rel]).wait_recv()
+            else:
+                for rel in range(1, n_dp):
+                    desc(ac.at[z, dp ^ rel], cut_s.at[0, rel], cut_r.at[0, rel]).wait_recv()
+                    desc(sg.at[z, dp ^ rel], cut_s.at[1, rel], cut_r.at[1, rel]).wait_recv()
+        for way in range(2):
+            sign = 1 - 2 * way
+            src = z - sign * h
+            nxt = z + sign
+            valid = (src >= 0) & (src < n_t)
+
+            def arrive(way=way, src=src, nxt=nxt):
+                if h:
+                    for at, s, r in line_parts(k):
+                        desc(at(src), s.at[way, h], r.at[way, h]).wait_recv()
+
+                if h + 1 < n_t:
+                    @pl.when((nxt >= 0) & (nxt < n_t))
+                    def _():
+                        for at, s, r in line_parts(k):
+                            send(at(src), at(src), s.at[way, h + 1], r.at[way, h + 1], dp, nxt)
+
+                if h or way == 0:
+                    pass_on(k, src)
+
+            if h:
+                pl.when(valid)(arrive)
+            else:
+                arrive()
+
+    tf = tile_of(ff, 512)
+
+    def matmul(k):
+        for s in range(n_t):
+            desc(og.at[k, 1 - core, s], sib_s.at[k, s], sib_r.at[k, s]).wait_recv()
+
+        def unpack(i, carry):
+            c, s, q = i // (n_t * chips), (i // chips) % n_t, i % chips
+            x = og[k, c, s, q].astype(F32)
+            to = (q * 2 + c) * n_t + s
+            lhs32[to, :, 0:half] = x[:rows]
+            lhs32[to, :, half:dk] = x[rows:]
+            return carry
+
+        lax.fori_loop(0, n_dp * n_t, unpack, 0)
+        lhs16[...] = lhs32[...].reshape(n_dp * group, dk).astype(BF16)
+
+        @pl.when(dp // 2 == k)
+        def _():
+            own32[...] = lhs32[:, :, pl.ds(pl.multiple_of((dp % 2) * half, half), half)].reshape(n_dp * group, half)
+
+        w_copies[k].wait()
+
+        def one(t, carry):
+            at = pl.ds(pl.multiple_of(t * tf, tf), tf)
+            part = jnp.dot(lhs16[...], wt[pl.ds(k * dk, dk), at], preferred_element_type=F32)
+            if k == 0:
+                acc[:, at] = part
+            else:
+                acc[:, at] += part
+            return carry
+
+        lax.fori_loop(0, ff // tf, one, 0)
+
+    start_gu()
+    start_cut()
+    for s in range(nk + n_t):
+        for h in range(n_t):
+            if 0 <= s - h <= nk:
+                step(s - h, h)
+        if s == n_t - 1:
+            for f in range(nf):
+                for j in range(2):
+                    gu_hop(j, f, 0)
+        if s == n_t:
+            for f in range(nf):
+                for j in range(2):
+                    gu_hop(j, f, 1)
+        if 0 <= s - (n_t - 1) < nk:
+            matmul(s - (n_t - 1))
+    grads_t_out[...] = own32[...].T.astype(BF16)
+
+    def unpack_cut(i, carry):
+        s, g = i // n_dp, i % n_dp
+        x = ac[s, g].astype(F32)
+        to = g * n_t + s
+        lhs32[to, :, 0:cols // 2] = x[:rows]
+        lhs32[to, :, cols // 2:cols] = x[rows:]
+        sg32[to] = sg[s, g]
+        return carry
+
+    lax.fori_loop(0, n_dp * n_t, unpack_cut, 0)
+    acts_t_out[...] = lhs32[:, :, 0:cols].reshape(n_dp * group, cols).T.astype(BF16)
+
+    eye = lax.broadcasted_iota(jnp.int32, (group, group), 0) == lax.broadcasted_iota(jnp.int32, (group, group), 1)
+    per = group // rows
+
+    def weigh(g, carry):
+        seg = sg32[pl.ds(g * per, per)].reshape(group, 128)[:, 0:1]
+        wide = jnp.broadcast_to(seg, (group, group))
+        row = jnp.sum(jnp.where(eye, wide, 0), axis=0, keepdims=True)
+        count = jnp.sum((wide == row).astype(F32), axis=1, keepdims=True)
+        wgt[g] = jnp.broadcast_to(1.0 / count, (group, 128))
+        return carry
+
+    lax.fori_loop(0, n_dp, weigh, 0)
+
+    for f in range(nf):
+        for j in range(2):
+            gu_hop(j, f, 2)
+    for f in range(nf):
+        for j in range(2):
+            a, b = gu_axes(j)
+            for t, slot in ((3, 0), (4, a), (5, b), (6, a ^ b)):
+                desc(gu.at[j, f, dp ^ CORE ^ slot], gu_s.at[j, f, t], gu_r.at[j, f, t]).wait_recv()
+    te = tile_of(fcut, 512)
+    for f in range(nf):
+        def element(i, carry, f=f):
+            g, t = i // (fcut // te), i % (fcut // te)
+            at = pl.ds(pl.multiple_of(t * te, te), te)
+            here = pl.ds(pl.multiple_of(f * fcut + t * te, te), te)
+            rows_at = pl.ds(pl.multiple_of(g * group, group), group)
+            gate = gu[0, f, g, :, at].astype(F32)
+            up = gu[1, f, g, :, at].astype(F32)
+            w = wgt[g][:, 0:1]
+            raw = acc[rows_at, here]
+            sigma = jax.nn.sigmoid(gate)
+            active = gate * sigma
+            hid = w * raw
+            gg_out[rows_at, here] = (hid * up * (sigma + active * (1.0 - sigma))).astype(BF16)
+            ug_out[rows_at, here] = (hid * active).astype(BF16)
+            wh_out[rows_at, here] = (w * active * up).astype(BF16)
+            return carry
+
+        lax.fori_loop(0, n_dp * (fcut // te), element, 0)
+
+    for k in range(nk):
+        for rel in range(1, chips):
+            desc(og.at[k, core, z, chip], og_s.at[k, rel], og_r.at[k, rel]).wait_send()
+        for s in range(n_t):
+            desc(og.at[k, core, s], sib_s.at[k, s], sib_r.at[k, s]).wait_send()
+    for rel in range(1, n_dp):
+        desc(acts_cut.at[dp ^ rel], cut_s.at[0, rel], cut_r.at[0, rel]).wait_send()
+        desc(sg.at[z, dp], cut_s.at[1, rel], cut_r.at[1, rel]).wait_send()
+    for k in range(nk + 1):
+        for h in range(1, n_t):
+            for way in range(2):
+                sign = 1 - 2 * way
+                src, nxt = z - sign * (h - 1), z + sign
+
+                @pl.when((src >= 0) & (src < n_t) & (nxt >= 0) & (nxt < n_t))
+                def _():
+                    for at, s, r in line_parts(k):
+                        desc(at(src), s.at[way, h], r.at[way, h]).wait_send()
+    for f in range(nf):
+        for j in range(2):
+            for t in range(7):
+                desc(gu.at[j, f, dp], gu_s.at[j, f, t], gu_r.at[j, f, t]).wait_send()
+
+
+def hidden_call(n_dp, n_t, acts, gate_pre, up_pre, out_grad, segments, down_weight):
+    rows, d = acts.shape
+    group, ff = gate_pre.shape
+    tokens = n_dp * group
+    chips = n_dp // 2
+    nk = chips
+    dk = d // nk
+    cols = d // n_dp
+    nf = 2
+    vmem, hbm = pl.BlockSpec(memory_space=pltpu.VMEM), pl.BlockSpec(memory_space=pltpu.HBM)
+    dma = pltpu.SemaphoreType.DMA
+    pairs = [(nk, chips), (nk, 2, n_t), (nk, n_t), (2, n_dp), (2, 2, n_t), (2, nf, 7)]
+    return pl.pallas_call(
+        functools.partial(hidden_kernel, n_dp, n_t),
+        out_shape=[jax.ShapeDtypeStruct((tokens, ff), BF16)] * 3
+        + [jax.ShapeDtypeStruct((cols, tokens), BF16)] * 2,
+        in_specs=[vmem, vmem, vmem, hbm, hbm, hbm],
+        out_specs=[vmem] * 5,
+        scratch_shapes=[
+            pltpu.VMEM((nk, 2, n_t, chips, 2 * rows, dk // 2), BF16),
+            pltpu.VMEM((n_dp, 2 * rows, cols // 2), BF16),
+            pltpu.VMEM((n_t, n_dp, 2 * rows, cols // 2), BF16),
+            pltpu.VMEM((n_t, n_dp, rows, 128), jnp.int32),
+            pltpu.VMEM((2, nf, n_dp, group, ff // nf), BF16),
+            pltpu.VMEM((d, ff), BF16),
+            pltpu.VMEM((tokens, ff), F32),
+            pltpu.VMEM((n_dp * n_t, rows, dk), F32),
+            pltpu.VMEM((tokens, dk), BF16),
+            pltpu.VMEM((tokens, cols), F32),
+            pltpu.VMEM((n_dp * n_t, rows, 128), jnp.int32),
+            pltpu.VMEM((n_dp, group, 128), F32),
+        ]
+        + [dma(shape) for shape in pairs for _ in range(2)]
+        + [dma((nk,)), dma((2, nf))],
+        compiler_params=pltpu.CompilerParams(
+            collective_id=0, has_side_effects=True, vmem_limit_bytes=58 * 2**20
+        ),
+        cost_estimate=pl.CostEstimate(
+            flops=2 * tokens * d * ff, bytes_accessed=2 * d * ff, transcendentals=tokens * ff
+        ),
+    )(acts, out_grad, segments, gate_pre, up_pre, down_weight)
+
+
+def outer_kernel(acts_t, grads_t, gg, ug, wh, gate_out, up_out, down_out):
+    gate_out[...] = jnp.dot(acts_t[...], gg[...], preferred_element_type=F32)
+    up_out[...] = jnp.dot(acts_t[...], ug[...], preferred_element_type=F32)
+    down_out[...] = jnp.dot(grads_t[...], wh[...], preferred_element_type=F32)
+
+
+def outer_call(gg, ug, wh, acts_t, grads_t):
+    cols, tokens = acts_t.shape
+    ff = gg.shape[1]
+    tf = tile_of(ff, 512)
+    left = pl.BlockSpec((cols, tokens), lambda i: (0, 0))
+    right = pl.BlockSpec((tokens, tf), lambda i: (0, i))
+    return pl.pallas_call(
+        outer_kernel,
+        grid=(ff // tf,),
+        out_shape=[jax.ShapeDtypeStruct((cols, ff), F32)] * 3,
+        in_specs=[left, left, right, right, right],
+        out_specs=[pl.BlockSpec((cols, tf), lambda i: (0, i))] * 3,
+        compiler_params=pltpu.CompilerParams(vmem_limit_bytes=60 * 2**20),
+        cost_estimate=pl.CostEstimate(
+            flops=6 * tokens * cols * ff, bytes_accessed=12 * cols * ff, transcendentals=0
+        ),
+    )(acts_t, grads_t, gg, ug, wh)
 
 
 def contract(left, right):
@@ -20,6 +379,10 @@
 def body(acts, gate_pre, up_pre, out_grad, segments, down_weight):
     n_dp, n_t = lax.axis_size("dp"), lax.axis_size("tensor")
     rows, d = acts.shape
+    if n_dp // 2 == 4:
+        return tuple(
+            outer_call(*hidden_call(n_dp, n_t, acts, gate_pre, up_pre, out_grad, segments, down_weight))
+        )
     grad_all = lax.all_gather(out_grad, MESH, axis=0, tiled=True)
     gate_all = lax.all_gather(gate_pre, "dp", axis=0, tiled=True)
     up_all = lax.all_gather(up_pre, "dp", axis=0, tiled=True)

time: 172 us -> 73.8 us (0.43)
  blocking collectives: 83.1 us -> 0 us
  Pallas kernels: 0 us -> 72.1 us
  matrix products: 36.6 us -> 0 us
  local copies, waits for them, and re-layouts: 17.7 us -> 0 us
  waiting for transfers between devices: 13.9 us -> 0 us
  between operations: 13.8 us -> 0.64 us
  starting transfers between devices: 5.3 us -> 0 us
    all_gather x2 -> x0, blocking collectives: 83.1 us -> none  [the longest x1 68.9 us: body(): seg_all = lax.all_gather(segments, MESH, axis=0, tiled=True)]
    pallas_call x0 -> x2, Pallas kernels: none -> 72.1 us  [the longest x1 61.5 us: hidden_call(): pl.pallas_call(functools.partial(hidden_kernel, n_dp, n_t), out_shape=[ja...]
    dot_general x4 -> x0, matrix products: 36.6 us -> none  [the longest x3 21.2 us: contract(): lax.dot_general(left, right, (((0,), (0,)), ((), ())), preferred_element_...]
    unnamed x6 -> x0, local copies, waits for them, and re-layouts: 17 us -> none
    all_gather x3 -> x0, waiting for transfers between devices: 11.8 us -> none  [the longest x1 11.8 us: body(): gate_all = lax.all_gather(gate_pre, 'dp', axis=0, tiled=True)]
    all_to_all x1 -> x0, starting transfers between devices: 5.18 us -> none  [body(): mine = lax.all_to_all(acts, 'dp', split_axis=1, concat_axis=0, tiled=True)]
    unnamed x3 -> x0, waiting for transfers between devices: 2.06 us -> none
  transfers between devices with their start and end apart: 4 -> 0, of which waited for: 1 -> 0; matrix products, arithmetic and copies ran while one was open for 10% -> 0% of each run, Pallas kernels for 0% -> 0%
where the time goes in v1:
time: 73.8 us; the launch traced here: 72.7 us
  Pallas kernels  72.1 us (98%)
    pallas_call x1, Pallas kernels, hidden_call(): pl.pallas_call(functools.partial(hidden_kernel, n_dp, n_t), out_shape=[ja...  61.5 us
    pallas_call x1, Pallas kernels, outer_call(): pl.pallas_call(outer_kernel, grid=(ff // tf,), out_shape=[jax.ShapeDtypeS...  10.6 us

profile of v1, /device:TPU:0, one launch (start us, length us, event | category | flops | bytes accessed | tf_op | source)
XLA Modules:
  0.0 72.7 jit_solution(2540720026713159499)
XLA Ops:
  0.6 61.5 %shard_map.85 = (bf16[256,3584]{1,0:T(8,128)(2,1)}, bf16[256,3584]{1,0:T(8,128)(2,1)}, bf16[256,3584]{1,0:T(8,128)(2,1)}, bf16[512,256]{1,0:T(8,128)(2,1)}, bf16[512,256]{1,0:T(8,128)(2,1)}) custom-call(bf16[8,4096]{1,0:T(8,128)(2,1)} %acts.1, bf16[8,4096]{1,0:T(8,128)(2,1)} %grads.1, s32[1,8]{1,0:T(1,128)} %segs.1, bf16[32,3584]{1,0:T(8,128)(2,1)} %gate_in.1, ...), custom_call_target="tpu_custom_call" | custom-call | flops 7516192768 | bytes 29360128 | tf_op jit(solution)/shard_map/pallas_call | solution.py:312
  62.1 10.6 %shard_map.86 = (f32[512,3584]{1,0:T(8,128)}, f32[512,3584]{1,0:T(8,128)}, f32[512,3584]{1,0:T(8,128)}) custom-call(bf16[512,256]{1,0:T(8,128)(2,1)} %get-tuple-element.8.acts_t, bf16[512,256]{1,0:T(8,128)(2,1)} %get-tuple-element.9.grads_t, bf16[256,3584]{1,0:T(8,128)(2,1)} %get-tuple-element.10.gg, bf16[256,3584]{1,0:T(8,128)(2,1)} %get-tuple-element.11.ug, ...), custom_call_target="tpu_custom_call" | custom-call | flops 2818572288 | bytes 22020096 | tf_op jit(solution)/shard_map/pallas_call | solution.py:355

commit v2 on v1

--- a/solution.py
+++ b/solution.py
@@ -21,7 +21,7 @@
     acts, grads, segs, gate_in, up_in, weight_in,
     gg_out, ug_out, wh_out, acts_t_out, grads_t_out,
     og, acts_cut, ac, sg, gu, wt, acc, lhs32, lhs16, own32, sg32, wgt,
-    og_s, og_r, line_s, line_r, sib_s, sib_r, cut_s, cut_r, cl_s, cl_r, gu_s, gu_r, w_sem, own_sem,
+    og_s, og_r, oz_s, oz_r, cut_s, cut_r, cl_s, cl_r, gu_s, gu_r, w_sem, own_sem,
 ):
     chips = n_dp // 2
     nk = chips
@@ -51,13 +51,8 @@
     for rel in range(1, n_dp):
         pl.semaphore_signal(barrier, inc=1, device_id=(dp ^ rel, z), device_id_type=pl.DeviceIdType.MESH)
 
-    @pl.when(z > 0)
-    def _():
-        pl.semaphore_signal(barrier, inc=1, device_id=(dp, z - 1), device_id_type=pl.DeviceIdType.MESH)
-
-    @pl.when(z < n_t - 1)
-    def _():
-        pl.semaphore_signal(barrier, inc=1, device_id=(dp, z + 1), device_id_type=pl.DeviceIdType.MESH)
+    for rel in range(1, n_t):
+        pl.semaphore_signal(barrier, inc=1, device_id=(dp, (z + rel) % n_t), device_id_type=pl.DeviceIdType.MESH)
 
     w_copies = [
         pltpu.make_async_copy(weight_in.at[pl.ds(k * dk, dk)], wt.at[pl.ds(k * dk, dk)], w_sem.at[k])
@@ -78,7 +73,7 @@
         return jnp.concatenate([x[:, :w], x[:, w:]], axis=0).astype(BF16)
 
     for k in range(nk):
-        og[k, core, z, chip] = stacked(grads[:, k * dk:(k + 1) * dk].astype(F32))
+        og[k, core, chip, z] = stacked(grads[:, k * dk:(k + 1) * dk].astype(F32))
     cols = d // n_dp
     for i in range(n_dp):
         acts_cut[i] = stacked(acts[:, i * cols:(i + 1) * cols].astype(F32))
@@ -88,94 +83,73 @@
     seg_col = jnp.sum(jnp.where(diag, seg_row, 0), axis=1, keepdims=True)
     sg[z, dp] = jnp.broadcast_to(seg_col, (rows, 128))
 
-    pl.semaphore_wait(barrier, n_dp - 1 + (z > 0).astype(jnp.int32) + (z < n_t - 1).astype(jnp.int32))
-
-    for k in range(nk):
-        for rel in range(1, chips):
-            mine = og.at[k, core, z, chip]
-            send(mine, mine, og_s.at[k, rel], og_r.at[k, rel], dp ^ (2 * rel), z)
-
-    def gu_axes(j):
-        return (NEAR, FAR) if j == 0 else (FAR, NEAR)
-
-    def start_gu():
-        for f in range(nf):
-            for j in range(2):
-                own_copies[j * nf + f].wait()
-            for t in range(2):
-                for j in range(2):
-                    mine = gu.at[j, f, dp]
-                    send(mine, mine, gu_s.at[j, f, t], gu_r.at[j, f, t], dp ^ gu_axes(j)[t], z)
-            for j in range(2):
-                mine = gu.at[j, f, dp]
-                send(mine, mine, gu_s.at[j, f, 3], gu_r.at[j, f, 3], dp ^ CORE, z)
-
-    def gu_hop(j, f, t):
-        a, b = gu_axes(j)
-        slot = gu.at[j, f, dp ^ (a, b, a ^ b)[t]]
-        desc(slot, gu_s.at[j, f, t], gu_r.at[j, f, t]).wait_recv()
-        if t == 0:
-            send(slot, slot, gu_s.at[j, f, 2], gu_r.at[j, f, 2], dp ^ b, z)
-        send(slot, slot, gu_s.at[j, f, 4 + t], gu_r.at[j, f, 4 + t], dp ^ CORE, z)
+    pl.semaphore_wait(barrier, n_dp + n_t - 2)
+
+    def start_lines():
+        for k in range(nk):
+            for rel in range(1, n_t):
+                mine = og.at[k, core, chip, z]
+                send(mine, mine, oz_s.at[k, rel], oz_r.at[k, rel], dp, (z + rel) % n_t)
 
     def start_cut():
         for rel in range(1, n_dp):
+            send(sg.at[z, dp], sg.at[z, dp], cut_s.at[1, rel], cut_r.at[1, rel], dp ^ rel, z)
+        for rel in range(1, n_dp):
             send(acts_cut.at[dp ^ rel], ac.at[z, dp], cut_s.at[0, rel], cut_r.at[0, rel], dp ^ rel, z)
-            send(sg.at[z, dp], sg.at[z, dp], cut_s.at[1, rel], cut_r.at[1, rel], dp ^ rel, z)
-
-    def line_parts(k):
-        if k < nk:
-            return [(lambda s: og.at[k, core, s], line_s.at[k], line_r.at[k])]
-        return [(lambda s: ac.at[s], cl_s.at[0], cl_r.at[0]), (lambda s: sg.at[s], cl_s.at[1], cl_r.at[1])]
-
-    def pass_on(k, s):
-        if k < nk:
-            plane = og.at[k, core, s]
-            send(plane, plane, sib_s.at[k, s], sib_r.at[k, s], dp ^ CORE, z)
-
-    def step(k, h):
-        if h == 0:
-            if k < nk:
-                for rel in range(1, chips):
-                    desc(og.at[k, core, z, chip ^ rel], og_s.at[k, rel], og_r.at[k, rel]).wait_recv()
-            else:
-                for rel in range(1, n_dp):
-                    desc(ac.at[z, dp ^ rel], cut_s.at[0, rel], cut_r.at[0, rel]).wait_recv()
-                    desc(sg.at[z, dp ^ rel], cut_s.at[1, rel], cut_r.at[1, rel]).wait_recv()
-        for way in range(2):
-            sign = 1 - 2 * way
-            src = z - sign * h
-            nxt = z + sign
-            valid = (src >= 0) & (src < n_t)
-
-            def arrive(way=way, src=src, nxt=nxt):
-                if h:
-                    for at, s, r in line_parts(k):
-                        desc(at(src), s.at[way, h], r.at[way, h]).wait_recv()
-
-                if h + 1 < n_t:
-                    @pl.when((nxt >= 0) & (nxt < n_t))
-                    def _():
-                        for at, s, r in line_parts(k):
-                            send(at(src), at(src), s.at[way, h + 1], r.at[way, h + 1], dp, nxt)
-
-                if h or way == 0:
-                    pass_on(k, src)
-
-            if h:
-                pl.when(valid)(arrive)
-            else:
-                arrive()
+
+    cut_parts = ((0, ac), (1, sg))
+
+    def cut_lines():
+        for i, ref in cut_parts:
+            for rel in range(1, n_dp):
+                desc(ref.at[z, dp ^ rel], cut_s.at[i, rel], cut_r.at[i, rel]).wait_recv()
+            for rel in range(1, n_t):
+                send(ref.at[z], ref.at[z], cl_s.at[i, rel], cl_r.at[i, rel], dp, (z + rel) % n_t)
+
+    def cut_arrived():
+        for i, ref in cut_parts:
+            for rel in range(1, n_t):
+                desc(ref.at[(z - rel + n_t) % n_t], cl_s.at[i, rel], cl_r.at[i, rel]).wait_recv()
+
+    def gu_part(j, f):
+        axes = (NEAR, FAR) if j == 0 else (FAR, NEAR)
+        return (lambda x: gu.at[j, f, x]), gu_s.at[j, f], gu_r.at[j, f], axes
+
+    def og_part(k):
+        axes = (NEAR, FAR) if k % 2 == 0 else (FAR, NEAR)
+        return (lambda x: og.at[k, x % 2, x // 2]), og_s.at[k], og_r.at[k], axes
+
+    def start_plane(part):
+        at, s, r, (a, b) = part
+        for t, to in ((0, a), (1, b), (3, CORE)):
+            send(at(dp), at(dp), s.at[t], r.at[t], dp ^ to, z)
+
+    def hop(part, t):
+        at, s, r, (a, b) = part
+        slot = at(dp ^ (a, b, a ^ b)[t])
+        desc(slot, s.at[t], r.at[t]).wait_recv()
+        if t == 0:
+            send(slot, slot, s.at[2], r.at[2], dp ^ b, z)
+        send(slot, slot, s.at[4 + t], r.at[4 + t], dp ^ CORE, z)
+
+    def from_sibling(part):
+        at, s, r, (a, b) = part
+        for t, slot in ((3, 0), (4, a), (5, b), (6, a ^ b)):
+            desc(at(dp ^ CORE ^ slot), s.at[t], r.at[t]).wait_recv()
+
+    def all_sent(part):
+        at, s, r, axes = part
+        for t in range(7):
+            desc(at(dp), s.at[t], r.at[t]).wait_send()
 
     tf = tile_of(ff, 512)
 
     def matmul(k):
-        for s in range(n_t):
-            desc(og.at[k, 1 - core, s], sib_s.at[k, s], sib_r.at[k, s]).wait_recv()
+        from_sibling(og_part(k))
 
         def unpack(i, carry):
-            c, s, q = i // (n_t * chips), (i // chips) % n_t, i % chips
-            x = og[k, c, s, q].astype(F32)
+            c, q, s = i // (n_t * chips), (i // n_t) % chips, i % n_t
+            x = og[k, c, q, s].astype(F32)
             to = (q * 2 + c) * n_t + s
             lhs32[to, :, 0:half] = x[:rows]
             lhs32[to, :, half:dk] = x[rows:]
@@ -201,23 +175,25 @@
 
         lax.fori_loop(0, ff // tf, one, 0)
 
-    start_gu()
+    gus = [gu_part(j, f) for f in range(nf) for j in range(2)]
+    ogs = [og_part(k) for k in range(nk)]
+    start_lines()
     start_cut()
-    for s in range(nk + n_t):
-        for h in range(n_t):
-            if 0 <= s - h <= nk:
-                step(s - h, h)
-        if s == n_t - 1:
-            for f in range(nf):
-                for j in range(2):
-                    gu_hop(j, f, 0)
-        if s == n_t:
-            for f in range(nf):
-                for j in range(2):
-                    gu_hop(j, f, 1)
-        if 0 <= s - (n_t - 1) < nk:
-            matmul(s - (n_t - 1))
-    grads_t_out[...] = own32[...].T.astype(BF16)
+    for c in own_copies:
+        c.wait()
+    for part in gus:
+        start_plane(part)
+    for k in range(nk):
+        for rel in range(1, n_t):
+            desc(og.at[k, core, chip, (z - rel + n_t) % n_t], oz_s.at[k, rel], oz_r.at[k, rel]).wait_recv()
+        start_plane(ogs[k])
+    cut_lines()
+    for t in range(2):
+        for part in gus:
+            hop(part, t)
+        for part in ogs:
+            hop(part, t)
+    cut_arrived()
 
     def unpack_cut(i, carry):
         s, g = i // n_dp, i % n_dp
@@ -244,16 +220,13 @@
 
     lax.fori_loop(0, n_dp, weigh, 0)
 
+    for part in gus:
+        hop(part, 2)
+    te = tile_of(fcut, 512)
     for f in range(nf):
         for j in range(2):
-            gu_hop(j, f, 2)
-    for f in range(nf):
-        for j in range(2):
-            a, b = gu_axes(j)
-            for t, slot in ((3, 0), (4, a), (5, b), (6, a ^ b)):
-                desc(gu.at[j, f, dp ^ CORE ^ slot], gu_s.at[j, f, t], gu_r.at[j, f, t]).wait_recv()
-    te = tile_of(fcut, 512)
-    for f in range(nf):
+            from_sibling(gus[f * 2 + j])
+
         def element(i, carry, f=f):
             g, t = i // (fcut // te), i % (fcut // te)
             at = pl.ds(pl.multiple_of(t * te, te), te)
@@ -262,39 +235,42 @@
             gate = gu[0, f, g, :, at].astype(F32)
             up = gu[1, f, g, :, at].astype(F32)
             w = wgt[g][:, 0:1]
-            raw = acc[rows_at, here]
             sigma = jax.nn.sigmoid(gate)
             active = gate * sigma
-            hid = w * raw
-            gg_out[rows_at, here] = (hid * up * (sigma + active * (1.0 - sigma))).astype(BF16)
-            ug_out[rows_at, here] = (hid * active).astype(BF16)
+            gg_out[rows_at, here] = (w * up * (sigma + active * (1.0 - sigma))).astype(BF16)
+            ug_out[rows_at, here] = (w * active).astype(BF16)
             wh_out[rows_at, here] = (w * active * up).astype(BF16)
             return carry
 
         lax.fori_loop(0, n_dp * (fcut // te), element, 0)
+        if f == 0:
+            for part in ogs:
+                hop(part, 2)
 
     for k in range(nk):
-        for rel in range(1, chips):
-            desc(og.at[k, core, z, chip], og_s.at[k, rel], og_r.at[k, rel]).wait_send()
-        for s in range(n_t):
-            desc(og.at[k, core, s], sib_s.at[k, s], sib_r.at[k, s]).wait_send()
+        matmul(k)
+    grads_t_out[...] = own32[...].T.astype(BF16)
+
+    def scale(i, carry):
+        at = pl.ds(pl.multiple_of(i * 128, 128), 128)
+        raw = acc[:, at]
+        gg_out[:, at] = (raw * gg_out[:, at].astype(F32)).astype(BF16)
+        ug_out[:, at] = (raw * ug_out[:, at].astype(F32)).astype(BF16)
+        return carry
+
+    lax.fori_loop(0, ff // 128, scale, 0)
+
+    for part in gus + ogs:
+        all_sent(part)
+    for k in range(nk):
+        for rel in range(1, n_t):
+            desc(og.at[k, core, chip, z], oz_s.at[k, rel], oz_r.at[k, rel]).wait_send()
     for rel in range(1, n_dp):
         desc(acts_cut.at[dp ^ rel], cut_s.at[0, rel], cut_r.at[0, rel]).wait_send()
         desc(sg.at[z, dp], cut_s.at[1, rel], cut_r.at[1, rel]).wait_send()
-    for k in range(nk + 1):
-        for h in range(1, n_t):
-            for way in range(2):
-                sign = 1 - 2 * way
-                src, nxt = z - sign * (h - 1), z + sign
-
-                @pl.when((src >= 0) & (src < n_t) & (nxt >= 0) & (nxt < n_t))
-                def _():
-                    for at, s, r in line_parts(k):
-                        desc(at(src), s.at[way, h], r.at[way, h]).wait_send()
-    for f in range(nf):
-        for j in range(2):
-            for t in range(7):
-                desc(gu.at[j, f, dp], gu_s.at[j, f, t], gu_r.at[j, f, t]).wait_send()
+    for i, ref in cut_parts:
+        for rel in range(1, n_t):
+            desc(ref.at[z], cl_s.at[i, rel], cl_r.at[i, rel]).wait_send()
 
 
 def hidden_call(n_dp, n_t, acts, gate_pre, up_pre, out_grad, segments, down_weight):
@@ -308,7 +284,7 @@
     nf = 2
     vmem, hbm = pl.BlockSpec(memory_space=pltpu.VMEM), pl.BlockSpec(memory_space=pltpu.HBM)
     dma = pltpu.SemaphoreType.DMA
-    pairs = [(nk, chips), (nk, 2, n_t), (nk, n_t), (2, n_dp), (2, 2, n_t), (2, nf, 7)]
+    pairs = [(nk, 7), (nk, n_t), (2, n_dp), (2, n_t), (2, nf, 7)]
     return pl.pallas_call(
         functools.partial(hidden_kernel, n_dp, n_t),
         out_shape=[jax.ShapeDtypeStruct((tokens, ff), BF16)] * 3
@@ -316,7 +292,7 @@
         in_specs=[vmem, vmem, vmem, hbm, hbm, hbm],
         out_specs=[vmem] * 5,
         scratch_shapes=[
-            pltpu.VMEM((nk, 2, n_t, chips, 2 * rows, dk // 2), BF16),
+            pltpu.VMEM((nk, 2, chips, n_t, 2 * rows, dk // 2), BF16),
             pltpu.VMEM((n_dp, 2 * rows, cols // 2), BF16),
             pltpu.VMEM((n_t, n_dp, 2 * rows, cols // 2), BF16),
             pltpu.VMEM((n_t, n_dp, rows, 128), jnp.int32),

time: 73.8 us -> 76.1 us (1.031); the launches traced: 72.7 us -> 75.8 us
  Pallas kernels: 72.1 us -> 75.1 us
    pallas_call x1, Pallas kernels: 61.5 us -> 64.6 us  [hidden_call(): pl.pallas_call(functools.partial(hidden_kernel, n_dp, n_t), out_shape=[ja...]
where the time goes in v2:
time: 76.1 us; the launch traced here: 75.8 us
  Pallas kernels  75.1 us (99%)
    pallas_call x1, Pallas kernels, hidden_call(): pl.pallas_call(functools.partial(hidden_kernel, n_dp, n_t), out_shape=[ja...  64.6 us
    pallas_call x1, Pallas kernels, outer_call(): pl.pallas_call(outer_kernel, grid=(ff // tf,), out_shape=[jax.ShapeDtypeS...  10.6 us

profile of v2, /device:TPU:0, one launch (start us, length us, event | category | flops | bytes accessed | tf_op | source)
XLA Modules:
  0.0 75.8 jit_solution(15535220126651961348)
XLA Ops:
  0.6 64.6 %shard_map.85 = (bf16[256,3584]{1,0:T(8,128)(2,1)}, bf16[256,3584]{1,0:T(8,128)(2,1)}, bf16[256,3584]{1,0:T(8,128)(2,1)}, bf16[512,256]{1,0:T(8,128)(2,1)}, bf16[512,256]{1,0:T(8,128)(2,1)}) custom-call(bf16[8,4096]{1,0:T(8,128)(2,1)} %acts.1, bf16[8,4096]{1,0:T(8,128)(2,1)} %grads.1, s32[1,8]{1,0:T(1,128)} %segs.1, bf16[32,3584]{1,0:T(8,128)(2,1)} %gate_in.1, ...), custom_call_target="tpu_custom_call" | custom-call | flops 7516192768 | bytes 29360128 | tf_op jit(solution)/shard_map/pallas_call | solution.py:288
  65.2 10.6 %shard_map.86 = (f32[512,3584]{1,0:T(8,128)}, f32[512,3584]{1,0:T(8,128)}, f32[512,3584]{1,0:T(8,128)}) custom-call(bf16[512,256]{1,0:T(8,128)(2,1)} %get-tuple-element.8.acts_t, bf16[512,256]{1,0:T(8,128)(2,1)} %get-tuple-element.9.grads_t, bf16[256,3584]{1,0:T(8,128)(2,1)} %get-tuple-element.10.gg, bf16[256,3584]{1,0:T(8,128)(2,1)} %get-tuple-element.11.ug, ...), custom_call_target="tpu_custom_call" | custom-call | flops 2818572288 | bytes 22020096 | tf_op jit(solution)/shard_map/pallas_call | solution.py:331

commit v3 on v1

--- a/solution.py
+++ b/solution.py
@@ -63,8 +63,6 @@
         pltpu.make_async_copy(weight_in.at[pl.ds(k * dk, dk)], wt.at[pl.ds(k * dk, dk)], w_sem.at[k])
         for k in range(nk)
     ]
-    for c in w_copies:
-        c.start()
     gu_in = (gate_in, up_in)
     own_copies = []
     for j in range(2):
@@ -201,8 +199,10 @@
 
         lax.fori_loop(0, ff // tf, one, 0)
 
+    start_cut()
     start_gu()
-    start_cut()
+    for c in w_copies:
+        c.start()
     for s in range(nk + n_t):
         for h in range(n_t):
             if 0 <= s - h <= nk:

time: 73.8 us -> 69.9 us (0.947)
  Pallas kernels: 72.1 us -> 68.1 us
    pallas_call x1, Pallas kernels: 61.5 us -> 57.6 us  [hidden_call(): pl.pallas_call(functools.partial(hidden_kernel, n_dp, n_t), out_shape=[ja...]
where the time goes in v3:
time: 69.9 us; the launch traced here: 68.8 us
  Pallas kernels  68.1 us (97%)
    pallas_call x1, Pallas kernels, hidden_call(): pl.pallas_call(functools.partial(hidden_kernel, n_dp, n_t), out_shape=[ja...  57.6 us
    pallas_call x1, Pallas kernels, outer_call(): pl.pallas_call(outer_kernel, grid=(ff // tf,), out_shape=[jax.ShapeDtypeS...  10.6 us

profile of v3, /device:TPU:0, one launch (start us, length us, event | category | flops | bytes accessed | tf_op | source)
XLA Modules:
  0.0 68.8 jit_solution(17343708635686514382)
XLA Ops:
  0.6 57.6 %shard_map.85 = (bf16[256,3584]{1,0:T(8,128)(2,1)}, bf16[256,3584]{1,0:T(8,128)(2,1)}, bf16[256,3584]{1,0:T(8,128)(2,1)}, bf16[512,256]{1,0:T(8,128)(2,1)}, bf16[512,256]{1,0:T(8,128)(2,1)}) custom-call(bf16[8,4096]{1,0:T(8,128)(2,1)} %acts.1, bf16[8,4096]{1,0:T(8,128)(2,1)} %grads.1, s32[1,8]{1,0:T(1,128)} %segs.1, bf16[32,3584]{1,0:T(8,128)(2,1)} %gate_in.1, ...), custom_call_target="tpu_custom_call" | custom-call | flops 7516192768 | bytes 29360128 | tf_op jit(solution)/shard_map/pallas_call | solution.py:312
  58.2 10.6 %shard_map.86 = (f32[512,3584]{1,0:T(8,128)}, f32[512,3584]{1,0:T(8,128)}, f32[512,3584]{1,0:T(8,128)}) custom-call(bf16[512,256]{1,0:T(8,128)(2,1)} %get-tuple-element.8.acts_t, bf16[512,256]{1,0:T(8,128)(2,1)} %get-tuple-element.9.grads_t, bf16[256,3584]{1,0:T(8,128)(2,1)} %get-tuple-element.10.gg, bf16[256,3584]{1,0:T(8,128)(2,1)} %get-tuple-element.11.ug, ...), custom_call_target="tpu_custom_call" | custom-call | flops 2818572288 | bytes 22020096 | tf_op jit(solution)/shard_map/pallas_call | solution.py:355
